TPU v7x, 32 devices: a whole 2x2x4 slice. The times are simulated.
32 devices in a mesh: blk: 4 (over y, core), inner: 8 (over z, x).
Axes of the slice: x: 2, y: 2, z: 4, core: 2. Of those that a mesh axis runs over, the one named last changes fastest.
Arguments:
- queries: bfloat16 [512, 1024], P(('blk', 'inner')), may hold values from -2 to 2
- passages: bfloat16 [512, 1024], P(('blk', 'inner')), may hold values from -2 to 2
- positive: int32 [512], P(('blk', 'inner')), may hold values from 0 to 511, as said below
- query_dups: int32 [512], P(('blk', 'inner')), may hold values from 0 to 127, as said below
- passage_dups: int32 [512], P(('blk', 'inner')), may hold values from 0 to 127, as said below
Outputs:
- query_grad: float32 [512, 1024], P(('blk', 'inner'))
- passage_grad: float32 [512, 1024], P(('blk', 'inner'))
- losses: float32 [512], P(('blk', 'inner'))
Inputs may be any that keep to these rules, and one draw needn't show every extreme that they name: Each passage is the positive passage of exactly one query. `query_dups`: a query and a passage, two queries or two passages with equal ids are duplicates of each other. `passage_dups`: ids share one range with query_dups.
All inputs are finite; a program needn't handle non-finite values.
Results may differ from a plain program's by a relative error of at most 0.0026.
Values may be sent and summed in bfloat16 or wider, within the bound.
A program may use at most 64 MiB of HBM per device.

v0:
```python
import jax
import jax.numpy as jnp
from jax import lax
from jax.sharding import PartitionSpec as P

SCALE = 50.0
NEGATIVE = -1e30


def joined(x, axis, combine):
    everything = jax.tree.map(lambda part: lax.all_gather(part, axis), x)
    initial = jax.tree.map(lambda part: part[0], everything)

    def step(k, so_far):
        return combine(so_far, jax.tree.map(lambda part: part[k], everything))

    return lax.fori_loop(1, lax.axis_size(axis), step, initial)


def pair_labels(blocks, per_device, total_queries, tables):
    all_pos, inverse, query_ids, passage_ids = tables
    local = blocks[:, None] * per_device + jnp.arange(per_device, dtype=jnp.int32)[None, :]
    row_ident = jnp.concatenate([local, local + total_queries], axis=1).reshape(-1)
    row_dup = jnp.concatenate([query_ids[local], passage_ids[local]], axis=1).reshape(-1)
    row_partner = jnp.concatenate([all_pos[local] + total_queries, inverse[local]], axis=1).reshape(
        -1
    )
    return (row_ident, row_dup, row_partner)


def tile_scores(columns, group_rows):
    return SCALE * lax.dot_general(
        columns, group_rows, (((1,), (1,)), ((), ())), preferred_element_type=jnp.float32
    )


def tile_masks(col_labels, row_labels):
    paired = col_labels[0][:, None] == row_labels[2][None, :]
    allowed = (col_labels[0][:, None] != row_labels[0][None, :]) & (
        (col_labels[1][:, None] != row_labels[1][None, :]) | paired
    )
    return (allowed, paired)


def side_stats(scores, allowed, paired, along):
    masked = jnp.where(allowed, scores, NEGATIVE)
    row_top = jnp.max(masked, axis=along)
    row_sum = jnp.sum(
        jnp.where(allowed, jnp.exp(masked - jnp.expand_dims(row_top, along)), 0.0), axis=along
    )
    row_pos = jnp.sum(jnp.where(paired, scores, 0.0), axis=along)
    return (row_top, row_sum, row_pos)


def combine(earlier, later):
    row_top = jnp.maximum(earlier[0], later[0])
    row_sum = earlier[1] * jnp.exp(earlier[0] - row_top) + later[1] * jnp.exp(later[0] - row_top)
    return (row_top, row_sum, earlier[2] + later[2])


def tile_weights(scores, allowed, paired, row_lse, row_c, col_lse, col_c):
    masked = jnp.where(allowed, scores, NEGATIVE)
    mixed = row_c[None, :] * jnp.exp(masked - row_lse[None, :]) + col_c[:, None] * jnp.exp(
        masked - col_lse[:, None]
    )
    return (jnp.where(allowed, mixed, 0.0) - paired.astype(jnp.float32)).astype(jnp.bfloat16)


def body(queries, passages, positive, query_dups, passage_dups):
    per_device = queries.shape[0]
    own_span = 2 * per_device
    blk_count = lax.axis_size("blk")
    inner_count = lax.axis_size("inner")
    blk_here = lax.axis_index("blk")
    inner_here = lax.axis_index("inner")
    own_rows = jnp.concatenate([queries, passages], 0)
    all_pos, query_ids, passage_ids = (
        lax.all_gather(positive, ("blk", "inner"), axis=0, tiled=True),
        lax.all_gather(query_dups, ("blk", "inner"), axis=0, tiled=True),
        lax.all_gather(passage_dups, ("blk", "inner"), axis=0, tiled=True),
    )
    total_queries = all_pos.shape[0]
    counter = jnp.arange(total_queries, dtype=jnp.int32)
    inverse = jnp.zeros((total_queries,), jnp.int32).at[all_pos].set(counter)
    tables = (all_pos, inverse, query_ids, passage_ids)
    group_rows = lax.all_gather(own_rows, "inner", axis=0, tiled=True)
    slot_index = jnp.arange(inner_count, dtype=jnp.int32)
    row_labels = pair_labels(blk_here * inner_count + slot_index, per_device, total_queries, tables)
    own_start = inner_here * own_span
    columns = lax.all_gather(own_rows, "blk", axis=0, tiled=True)
    col_blocks = jnp.arange(blk_count, dtype=jnp.int32) * inner_count + inner_here
    col_labels = pair_labels(col_blocks, per_device, total_queries, tables)
    scores = tile_scores(columns, group_rows)
    allowed, paired = tile_masks(col_labels, row_labels)
    row_stats = side_stats(scores, allowed, paired, 0)
    row_top, row_sum, row_pos = joined((row_stats[0], row_stats[1], row_stats[2]), "inner", combine)
    group_lse = row_top + jnp.log(row_sum)
    every_lse = lax.all_gather(group_lse, "blk", axis=0, tiled=True)
    arranged = every_lse.reshape(blk_count * inner_count, 2, per_device)
    lse_query = arranged[:, 0, :].reshape(-1)
    lse_passage = arranged[:, 1, :].reshape(-1)
    pair_total = jnp.logaddexp(lse_query, lse_passage[all_pos])
    lse_table = jnp.concatenate([lse_query, lse_passage])
    weight_table = jnp.concatenate(
        [jnp.exp(lse_query - pair_total), jnp.exp(lse_passage - pair_total[inverse])]
    )
    own_block = blk_here * inner_count + inner_here
    losses = lax.dynamic_slice_in_dim(
        pair_total, own_block * per_device, per_device
    ) - lax.dynamic_slice_in_dim(row_pos, own_start, per_device)
    weights = tile_weights(
        scores,
        allowed,
        paired,
        lse_table[row_labels[0]],
        weight_table[row_labels[0]],
        lse_table[col_labels[0]],
        weight_table[col_labels[0]],
    )
    gradient = lax.psum_scatter(
        SCALE
        * lax.dot_general(
            weights, columns, (((0,), (0,)), ((), ())), preferred_element_type=jnp.float32
        ),
        "inner",
        scatter_dimension=0,
        tiled=True,
    )
    return (gradient[:per_device], gradient[per_device:], losses)


def solution(mesh):
    in_specs = (
        P(("blk", "inner"), None),
        P(("blk", "inner"), None),
        P(("blk", "inner")),
        P(("blk", "inner")),
        P(("blk", "inner")),
    )
    out_specs = (P(("blk", "inner"), None), P(("blk", "inner"), None), P(("blk", "inner")))
    return jax.shard_map(body, mesh=mesh, in_specs=in_specs, out_specs=out_specs, check_vma=False)
```

profile of v0, /device:TPU:0, one launch (start us, length us, event | category | flops | bytes accessed | tf_op | source)
XLA Modules:
  0.0 244.5 jit_solution(10532761888391303217)
XLA Ops:
  7.2 0.0 reduce-scatter.2.cloned.1.call-start
  7.2 0.1 compare_select_fusion.5
  7.3 0.1 iota_add_fusion.1
  7.4 0.1 pad_add_fusion.3
  7.5 0.1 ne.37
  7.5 0.1 reshape.174
  7.6 0.1 reshape.177
  7.7 0.7 copy-done.2
  8.4 0.2 dynamic-update-slice.1
  8.6 0.7 copy-done.3
  9.2 0.2 dynamic-update-slice.2
  9.4 0.7 copy-done.4
  10.0 0.2 dynamic-update-slice
  10.2 42.0 %all-reduce.3 = (s32[512]{0:T(512)S(1)}, s32[512]{0:T(512)S(1)}, s32[512]{0:T(512)S(1)}) all-reduce(s32[512]{0:T(512)S(1)} %dynamic-update-slice.2, s32[512]{0:T(512)S(1)} %dynamic-update-slice.1, s32[512]{0:T(512)S(1)} %dynamic-update-slice), channel_id=1, replica_groups=mesh['blk'=4,'inner'=8] {'blk','inner'}, use_global_device_ids=true, to_apply=%add.2 | all-reduce | flops 1536 | bytes 12288
  52.3 2.4 scatter_custom_fusion
  54.7 0.1 compare_select_fusion.1
  54.8 0.1 reshape.193
  54.9 1.3 gather_fusion.5
  56.2 1.3 gather_fusion.4
  57.5 1.3 gather_fusion.2
  58.7 0.8 gather_fusion
  59.5 0.8 gather_fusion.1
  60.3 1.3 gather_fusion.3
  61.6 0.1 iota_add_fusion
  61.7 0.1 pad_add_fusion
  61.8 0.1 ne.39
  61.8 0.1 reshape.173
  61.9 0.4 copy-done
  62.4 0.8 copy-done.1
  63.1 6.5 %all_gather.39 = bf16[128,1024]{1,0:T(8,128)(2,1)S(1)} all-gather(bf16[32,1024]{1,0:T(8,128)(2,1)S(1)} %constant_dynamic-update-slice_fusion), channel_id=1, replica_groups=mesh['blk'=4,'inner'=8] {'blk'}, dimensions={0}, use_global_device_ids=true | all-gather | bytes 327680 | tf_op jit(solution)/shard_map/all_gather | solution.py:90
  69.6 31.5 %all_gather.40 = bf16[256,1024]{1,0:T(8,128)(2,1)S(1)} all-gather(bf16[32,1024]{1,0:T(8,128)(2,1)S(1)} %constant_dynamic-update-slice_fusion), channel_id=1, replica_groups=mesh['blk'=4,'inner'=8] {'inner'}, dimensions={0}, use_global_device_ids=true | all-gather | bytes 589824 | tf_op jit(solution)/shard_map/all_gather | solution.py:86
  101.1 0.1 reshape.176
  101.2 0.1 reshape.184
  101.3 0.1 pad_add_fusion.4
  101.4 0.1 ne.42
  101.5 0.1 reshape.200
  101.5 0.1 reshape.192
  101.6 0.1 pad_add_fusion.1
  101.7 0.1 ne.44
  101.8 0.1 reshape.298
  101.9 0.1 reshape.216
  101.9 0.1 pad_add_fusion.2
  102.0 0.1 eq.6
  102.1 0.3 fusion.10
  102.4 0.1 fusion
  102.6 19.5 %all-gather.4 = f32[8,1,256]{2,1,0:T(1,128)S(1)} all-gather(f32[1,1,256]{2,1,0:T(1,128)S(1)} %bitcast.47), channel_id=3, replica_groups=mesh['blk'=4,'inner'=8] {'inner'}, dimensions={0}, use_global_device_ids=true | all-gather | bytes 9216 | tf_op jit(solution)/shard_map/all_gather | solution.py:11
  122.1 16.3 %all-gather.5 = f32[8,1,256]{2,1,0:T(1,128)S(1)} all-gather(f32[1,1,256]{2,1,0:T(1,128)S(1)} %bitcast.46), channel_id=4, replica_groups=mesh['blk'=4,'inner'=8] {'inner'}, dimensions={0}, use_global_device_ids=true | all-gather | bytes 9216 | tf_op jit(solution)/shard_map/all_gather | solution.py:11
  138.3 18.3 %all-gather.3 = f32[8,1,256]{2,1,0:T(1,128)S(1)} all-gather(f32[1,1,256]{2,1,0:T(1,128)S(1)} %bitcast.45), channel_id=2, replica_groups=mesh['blk'=4,'inner'=8] {'inner'}, dimensions={0}, use_global_device_ids=true | all-gather | bytes 9216 | tf_op jit(solution)/shard_map/all_gather | solution.py:11
  156.6 0.6 while.19
  157.3 5.1 %all-gather.6 = f32[4,1,256]{2,1,0:T(1,128)S(1)} all-gather(f32[1,1,256]{2,1,0:T(1,128)S(1)} %bitcast.48), channel_id=1, replica_groups=mesh['blk'=4,'inner'=8] {'blk'}, dimensions={0}, use_global_device_ids=true | all-gather | bytes 5120 | tf_op jit(solution)/shard_map/all_gather | solution.py:98
  162.3 0.1 reshape.172
  162.5 0.1 slice_reduce_fusion
  162.6 0.1 reshape_squeeze.7
  162.6 0.1 reshape_squeeze.6
  162.7 3.5 %gather_fusion.6 = f32[512]{0:T(512)S(1)} fusion(f32[512]{0:T(512)S(1)} %reshape_squeeze.7, s32[1024]{0:T(1024)S(1)} %get-tuple-element.225), kind=kCustom, calls=%fused_computation.6 | custom fusion | bytes 6144 | tf_op jit(solution)/shard_map/gather | solution.py:102
  166.3 3.5 %gather_fusion.7 = f32[512]{0:T(512)S(1)} fusion(f32[512]{0:T(512)S(1)} %get-tuple-element.212, s32[1024]{0:T(1024)S(1)} %get-tuple-element.224), kind=kCustom, calls=%fused_computation.7 | custom fusion | bytes 6144 | tf_op jit(solution)/shard_map/gather | solution.py:105
  169.8 1.0 gather_fusion.10
  170.8 1.0 gather_fusion.11
  171.8 1.4 gather_fusion.9
  173.2 1.4 gather_fusion.8
  174.5 1.5 convolution_multiply_fusion
  176.0 0.6 dynamic-slice_subtract_fusion
  176.6 59.6 %reduce-scatter.2.cloned.1.call-done = f32[32,1024]{1,0:T(8,128)} async-done(((f32[256,1024]{1,0:T(8,128)}), f32[32,1024]{1,0:T(8,128)}) %reduce-scatter.2.cloned.1.call-update) | async-done | bytes 131088 | tf_op jit(solution)/shard_map/reduce_scatter | solution.py:120
  236.2 1.5 fusion.19
  (62 shorter events, 0.5 us)
Async XLA Ops:
  7.2 229.0 %reduce-scatter.2.cloned.1.call-start = ((), (), s32[]{:S(2)}) async-start(), calls=%async_computation.1 | async-start | bytes 1179648 | tf_op jit(solution)/shard_map/reduce_scatter | solution.py:120
  7.7 0.7 copy-start.2
  8.6 0.7 copy-start.3
  9.4 0.7 copy-start.4
  61.6 0.8 copy-start
  62.4 0.8 copy-start.1
Sparse Core Ops, SparseCore 0:
  176.1 59.9 reduce-scatter.1
where the time goes:
time: 245 us
  blocking collectives  139 us (57%)
  waiting for transfers between devices  59.6 us (24%)
  local copies, waits for them, and re-layouts  27.8 us (11%)
  between operations  14.3 us (6%)
    reduce_scatter x1, waiting for transfers between devices, body(): lax.psum_scatter(SCALE * lax.dot_general(weights, columns, (((0,), (0,)),...  59.6 us
    all_gather x3, blocking collectives, joined(): everything = jax.tree.map(lambda part: lax.all_gather(part, axis), x)  54 us
    unnamed x1, blocking collectives  42 us
    all_gather x1, blocking collectives, body(): group_rows = lax.all_gather(own_rows, 'inner', axis=0, tiled=True)  31.5 us
    all_gather x1, blocking collectives, body(): columns = lax.all_gather(own_rows, 'blk', axis=0, tiled=True)  6.51 us
    all_gather x1, blocking collectives, body(): every_lse = lax.all_gather(group_lse, 'blk', axis=0, tiled=True)  5.07 us
  transfers between devices with their start and end apart: 1, of which 1 were waited for; matrix products, arithmetic and copies ran while one was open for 0% of the time, Pallas kernels for 0%

commit v1 on v0

--- a/solution.py
+++ b/solution.py
@@ -1,6 +1,10 @@
+import functools
+
 import jax
 import jax.numpy as jnp
 from jax import lax
+from jax.experimental import pallas as pl
+from jax.experimental.pallas import tpu as pltpu
 from jax.sharding import PartitionSpec as P
 
 SCALE = 50.0
@@ -129,6 +133,321 @@
     return (gradient[:per_device], gradient[per_device:], losses)
 
 
+LANES = 128
+
+
+def fits_kernel(blk_count, inner_count):
+    lines = inner_count // 2
+    return blk_count == 4 and inner_count % 2 == 0 and lines & (lines - 1) == 0 and lines <= 8
+
+
+def swapped(value, distance):
+    result = value
+    bit = 1
+    while bit <= distance:
+        if distance & bit:
+            result = result + bit - 2 * bit * (lax.div(value, bit) % 2)
+        bit *= 2
+    return result
+
+
+def lane_sum(parts):
+    total = parts[0]
+    for part in parts[1:]:
+        total = total + part
+    return total
+
+
+def fused_kernel(
+    blk_count,
+    inner_count,
+    per_device,
+    q_ref,
+    p_ref,
+    pos_ref,
+    qd_ref,
+    pd_ref,
+    qg_ref,
+    pg_ref,
+    loss_ref,
+    rows,
+    label_out,
+    labels,
+    lse_out,
+    lses,
+    load_sem,
+    row_send,
+    row_recv,
+    label_send,
+    label_recv,
+    lse_send,
+    lse_recv,
+):
+    device_count = blk_count * inner_count
+    span = 2 * per_device
+    total_rows = device_count * span
+    total_queries = total_rows // 2
+    per_lanes = LANES // span
+    groups = device_count // per_lanes
+    lines = inner_count // 2
+
+    blk = lax.axis_index("blk")
+    inner = lax.axis_index("inner")
+    core, y = blk % 2, lax.div(blk, 2)
+    x, z = inner % 2, lax.div(inner, 2)
+    me = blk * inner_count + inner
+    sibling = (blk + 1 - 2 * core, inner)
+    x_peer = (blk, inner + 1 - 2 * x)
+    y_peer = ((1 - y) * 2 + core, inner)
+
+    def block_of(device):
+        return device[0] * inner_count + device[1]
+
+    def at_line(device, z_there):
+        return (device[0], z_there * 2 + device[1] % 2)
+
+    def whole(block):
+        return rows.at[pl.ds(pl.multiple_of(block * span, span), span)]
+
+    def half(block, k):
+        start = pl.multiple_of(block * span + k * per_device, per_device)
+        return rows.at[pl.ds(start, per_device)]
+
+    loads = [
+        pltpu.make_async_copy(q_ref, half(me, 0), load_sem.at[0]),
+        pltpu.make_async_copy(p_ref, half(me, 1), load_sem.at[1]),
+    ]
+    for copy in loads:
+        copy.start()
+
+    barrier = pltpu.get_barrier_semaphore()
+
+    def greet(d, carry):
+        target = lax.rem(me + d, device_count)
+        pl.semaphore_signal(
+            barrier,
+            inc=1,
+            device_id=(lax.div(target, inner_count), lax.rem(target, inner_count)),
+            device_id_type=pl.DeviceIdType.MESH,
+        )
+        return carry
+
+    lax.fori_loop(1, device_count, greet, 0)
+
+    lane = lax.broadcasted_iota(jnp.int32, (1, LANES), 1)
+    own_place = lax.div(lane, span) == lax.rem(me, per_lanes)
+    lane_here = lax.rem(lane, span)
+    code_row = jnp.zeros((1, LANES), jnp.int32)
+    dup_row = jnp.zeros((1, LANES), jnp.int32)
+    for k in range(per_device):
+        code_row = jnp.where(lane_here == k, pos_ref[k], code_row)
+        dup_row = jnp.where(lane_here == k, qd_ref[k], dup_row)
+        dup_row = jnp.where(lane_here == per_device + k, pd_ref[k], dup_row)
+    passage_lane = lane_here >= per_device
+    code_row = jnp.where(
+        passage_lane, me * per_device + lane_here - per_device + total_queries, code_row
+    )
+    label_out[0:1, :] = jnp.where(own_place, code_row, 0)
+    label_out[1:2, :] = jnp.where(own_place, dup_row, 0)
+
+    pl.semaphore_wait(barrier, device_count - 1)
+    for copy in loads:
+        copy.wait()
+
+    sent = []
+
+    def send(ref, device, recv):
+        copy = pltpu.make_async_remote_copy(
+            src_ref=ref,
+            dst_ref=ref,
+            send_sem=row_send.at[len(sent)],
+            recv_sem=recv,
+            device_id=device,
+            device_id_type=pl.DeviceIdType.MESH,
+        )
+        copy.start()
+        sent.append(copy)
+
+    def arrived(ref, sem):
+        pltpu.make_async_copy(ref, ref, sem).wait()
+
+    def spread(block):
+        send(whole(block), x_peer, row_recv.at[block, 0])
+        send(whole(block), y_peer, row_recv.at[block, 0])
+
+    def to_sibling(block):
+        send(whole(block), sibling, row_recv.at[block, 0])
+
+    spread(me)
+    for d in range(1, lines):
+        send(whole(me), at_line((blk, inner), swapped(z, d)), row_recv.at[me, 0])
+    to_sibling(me)
+
+    own_labels = pltpu.make_async_copy(label_out, labels.at[me], label_recv)
+    own_labels.start()
+
+    def send_small(out, into, send_sem, recv_sem):
+        def step(d, carry):
+            target = lax.rem(me + d, device_count)
+            pltpu.make_async_remote_copy(
+                src_ref=out,
+                dst_ref=into.at[me],
+                send_sem=send_sem,
+                recv_sem=recv_sem,
+                device_id=(lax.div(target, inner_count), lax.rem(target, inner_count)),
+                device_id_type=pl.DeviceIdType.MESH,
+            ).start()
+            return carry
+
+        lax.fori_loop(1, device_count, step, 0)
+
+    send_small(label_out, labels, label_send, label_recv)
+
+    for step in range(lines + 2):
+        if 1 <= step < lines:
+            block = block_of(at_line((blk, inner), swapped(z, step)))
+            arrived(whole(block), row_recv.at[block, 0])
+            spread(block)
+            to_sibling(block)
+        if 1 <= step <= lines:
+            there = swapped(z, step - 1)
+            block = block_of(at_line(x_peer, there))
+            arrived(whole(block), row_recv.at[block, 0])
+            send(half(block, 0), y_peer, row_recv.at[block, 0])
+            to_sibling(block)
+            block = block_of(at_line(y_peer, there))
+            arrived(whole(block), row_recv.at[block, 0])
+            send(half(block, 1), x_peer, row_recv.at[block, 1])
+            to_sibling(block)
+        if step >= 2:
+            block = block_of(at_line((y_peer[0], x_peer[1]), swapped(z, step - 2)))
+            arrived(half(block, 0), row_recv.at[block, 0])
+            arrived(half(block, 1), row_recv.at[block, 1])
+            to_sibling(block)
+
+    arrived(labels, label_recv)
+    codes = [
+        lane_sum([labels[g * per_lanes + k][0:1, :] for k in range(per_lanes)])
+        for g in range(groups)
+    ]
+    dups = [
+        lane_sum([labels[g * per_lanes + k][1:2, :] for k in range(per_lanes)])
+        for g in range(groups)
+    ]
+    code_lanes = jnp.concatenate(codes, axis=1)
+    dup_lanes = jnp.concatenate(dups, axis=1)
+    partner_lanes = jnp.where(
+        code_lanes >= total_queries, code_lanes - total_queries, code_lanes + total_queries
+    )
+    sub = lax.broadcasted_iota(jnp.int32, (span, LANES), 0)
+    lane2 = lax.broadcasted_iota(jnp.int32, (span, LANES), 1)
+    diagonal = lane2 == sub + lax.rem(me, per_lanes) * span
+    code_col = jnp.sum(jnp.where(diagonal, label_out[0:1, :], 0), axis=1, keepdims=True)
+    dup_col = jnp.sum(jnp.where(diagonal, label_out[1:2, :], 0), axis=1, keepdims=True)
+    paired = code_col == partner_lanes
+    allowed = (code_col != code_lanes) & ((dup_col != dup_lanes) | paired)
+
+    for z_there in range(lines):
+        for y_there in range(blk_count // 2):
+            for x_there in range(2):
+                block = block_of(((2 * y_there + 1 - core), z_there * 2 + x_there))
+                arrived(whole(block), row_recv.at[block, 0])
+
+    own = whole(me)[...]
+    scores = SCALE * lax.dot_general(
+        own, rows[...], (((1,), (1,)), ((), ())), preferred_element_type=jnp.float32
+    )
+    masked = jnp.where(allowed, scores, NEGATIVE)
+    top = jnp.max(masked, axis=1, keepdims=True)
+    total = jnp.sum(jnp.where(allowed, jnp.exp(masked - top), 0.0), axis=1, keepdims=True)
+    positive_score = jnp.sum(jnp.where(paired, scores, 0.0), axis=1, keepdims=True)
+    lse = top + jnp.log(total)
+    lse_out[...] = jnp.sum(jnp.where(diagonal, lse, 0.0), axis=0, keepdims=True)
+
+    own_lse = pltpu.make_async_copy(lse_out, lses.at[me], lse_recv)
+    own_lse.start()
+    send_small(lse_out, lses, lse_send, lse_recv)
+    code_cols = jnp.transpose(jnp.concatenate(codes, axis=0))
+    arrived(lses, lse_recv)
+
+    lse_rows = [
+        lane_sum([lses[g * per_lanes + k] for k in range(per_lanes)]) for g in range(groups)
+    ]
+    lse_lanes = jnp.concatenate(lse_rows, axis=1)
+    lse_cols = jnp.transpose(jnp.concatenate(lse_rows, axis=0))
+    found = jnp.zeros((8, total_rows), jnp.float32)
+    for g in range(groups):
+        match = code_cols[:, g : g + 1] == partner_lanes
+        picked = jnp.where(match, lse_cols[:, g : g + 1], 0.0)
+        found = found + jnp.sum(picked.reshape(LANES // 8, 8, total_rows), axis=0)
+    partner_lse = jnp.sum(found, axis=0, keepdims=True)
+
+    def added(a, b):
+        return jnp.maximum(a, b) + jnp.log(1.0 + jnp.exp(-jnp.abs(a - b)))
+
+    pair_lanes = added(lse_lanes, partner_lse)
+    pair_col = jnp.sum(jnp.where(paired, pair_lanes, 0.0), axis=1, keepdims=True)
+    losses = pair_col - positive_score
+    place = lax.broadcasted_iota(jnp.int32, (span, LANES), 0) == lax.broadcasted_iota(
+        jnp.int32, (span, LANES), 1
+    )
+    loss_ref[...] = jnp.sum(jnp.where(place, losses, 0.0), axis=0, keepdims=True)
+    mixed = jnp.exp(masked - pair_col) + jnp.exp(masked - pair_lanes)
+    weights = jnp.where(allowed, mixed, 0.0) - paired.astype(jnp.float32)
+    gradient = SCALE * lax.dot_general(
+        weights.astype(jnp.bfloat16),
+        rows[...],
+        (((1,), (0,)), ((), ())),
+        preferred_element_type=jnp.float32,
+    )
+    qg_ref[...] = gradient[:per_device]
+    pg_ref[...] = gradient[per_device:]
+
+    for copy in sent:
+        copy.wait_send()
+    arrived(labels.at[pl.ds(0, device_count - 1)], label_send)
+    arrived(lses.at[pl.ds(0, device_count - 1)], lse_send)
+
+
+def fused_body(blk_count, inner_count, queries, passages, positive, query_dups, passage_dups):
+    per_device, width = queries.shape
+    device_count = blk_count * inner_count
+    span = 2 * per_device
+    sends = (inner_count // 2) * 9 + 8
+    vmem = pl.BlockSpec(memory_space=pltpu.VMEM)
+    smem = pl.BlockSpec(memory_space=pltpu.SMEM)
+    hbm = pl.BlockSpec(memory_space=pl.ANY)
+    query_grad, passage_grad, losses = pl.pallas_call(
+        functools.partial(fused_kernel, blk_count, inner_count, per_device),
+        out_shape=(
+            jax.ShapeDtypeStruct((per_device, width), jnp.float32),
+            jax.ShapeDtypeStruct((per_device, width), jnp.float32),
+            jax.ShapeDtypeStruct((1, LANES), jnp.float32),
+        ),
+        in_specs=[hbm, hbm, smem, smem, smem],
+        out_specs=[vmem, vmem, vmem],
+        scratch_shapes=[
+            pltpu.VMEM((device_count * span, width), jnp.bfloat16),
+            pltpu.VMEM((2, LANES), jnp.int32),
+            pltpu.VMEM((device_count, 2, LANES), jnp.int32),
+            pltpu.VMEM((1, LANES), jnp.float32),
+            pltpu.VMEM((device_count, 1, LANES), jnp.float32),
+            pltpu.SemaphoreType.DMA((2,)),
+            pltpu.SemaphoreType.DMA((sends,)),
+            pltpu.SemaphoreType.DMA((device_count, 2)),
+            pltpu.SemaphoreType.DMA,
+            pltpu.SemaphoreType.DMA,
+            pltpu.SemaphoreType.DMA,
+            pltpu.SemaphoreType.DMA,
+        ],
+        compiler_params=pltpu.CompilerParams(
+            collective_id=0, has_side_effects=True, vmem_limit_bytes=32 * 1024 * 1024
+        ),
+        name="contrastive",
+    )(queries, passages, positive, query_dups, passage_dups)
+    return query_grad, passage_grad, losses[0, :per_device]
+
+
 def solution(mesh):
     in_specs = (
         P(("blk", "inner"), None),
@@ -138,4 +457,8 @@
         P(("blk", "inner")),
     )
     out_specs = (P(("blk", "inner"), None), P(("blk", "inner"), None), P(("blk", "inner")))
-    return jax.shard_map(body, mesh=mesh, in_specs=in_specs, out_specs=out_specs, check_vma=False)
+    part = body
+    blk_count, inner_count = mesh.shape["blk"], mesh.shape["inner"]
+    if fits_kernel(blk_count, inner_count):
+        part = functools.partial(fused_body, blk_count, inner_count)
+    return jax.shard_map(part, mesh=mesh, in_specs=in_specs, out_specs=out_specs, check_vma=False)

time: 245 us -> 36.7 us (0.15)
  blocking collectives: 139 us -> 0 us
  waiting for transfers between devices: 59.6 us -> 0 us
  Pallas kernels: 0 us -> 30.5 us
  local copies, waits for them, and re-layouts: 27.8 us -> 5.24 us
  between operations: 14.3 us -> 0.65 us
    all_gather x6 -> x0, blocking collectives: 97.1 us -> none  [the longest x3 54 us: joined(): everything = jax.tree.map(lambda part: lax.all_gather(part, axis), x)]
    reduce_scatter x1 -> x0, waiting for transfers between devices: 59.6 us -> none  [body(): lax.psum_scatter(SCALE * lax.dot_general(weights, columns, (((0,), (0,)),...]
    unnamed x1 -> x0, blocking collectives: 42 us -> none
    pallas_call x0 -> x1, Pallas kernels: none -> 30.5 us  [fused_body(): pl.pallas_call(functools.partial(fused_kernel, blk_count, inner_count, pe...]
    gather x17 -> x0, local copies, waits for them, and re-layouts: 18.8 us -> none  [the longest x1 3.51 us: body(): pair_total[inverse]]
  transfers between devices with their start and end apart: 1 -> 0, of which waited for: 1 -> 0; matrix products, arithmetic and copies ran while one was open for 0% -> 0% of each run, Pallas kernels for 0% -> 0%
where the time goes in v1:
time: 36.7 us; the launch traced here: 36.4 us
  Pallas kernels  30.5 us (83%)
  local copies, waits for them, and re-layouts  5.24 us (14%)
  between operations  0.65 us (2%)
    pallas_call x1, Pallas kernels, fused_body(): pl.pallas_call(functools.partial(fused_kernel, blk_count, inner_count, pe...  30.5 us
    unnamed x12, local copies, waits for them, and re-layouts  4.73 us

profile of v1, /device:TPU:0, one launch (start us, length us, event | category | flops | bytes accessed | tf_op | source)
XLA Modules:
  0.0 36.4 jit_solution(9649311944806306810)
XLA Ops:
  0.6 0.0 copy-start
  0.6 0.7 %copy-done = bf16[16,1024]{1,0:T(8,128)(2,1)S(1)} copy-done((bf16[16,1024]{1,0:T(8,128)(2,1)S(1)}, bf16[16,1024]{1,0:T(8,128)(2,1)}, u32[]{:S(2)}) %copy-start) | copy-done | bytes 32792
  1.4 0.0 copy-start.1
  1.4 0.8 %copy-done.1 = bf16[16,1024]{1,0:T(8,128)(2,1)S(1)} copy-done((bf16[16,1024]{1,0:T(8,128)(2,1)S(1)}, bf16[16,1024]{1,0:T(8,128)(2,1)}, u32[]{:S(2)}) %copy-start.1) | copy-done | bytes 32792
  2.1 0.0 copy-start.2
  2.2 0.7 %copy-done.2 = s32[16]{0:T(128)S(1)} copy-done((s32[16]{0:T(128)S(1)}, s32[16]{0:T(128)}, u32[]{:S(2)}) %copy-start.2) | copy-done | bytes 88
  2.8 0.0 copy-start.3
  2.8 0.7 %copy-done.3 = s32[16]{0:T(128)S(1)} copy-done((s32[16]{0:T(128)S(1)}, s32[16]{0:T(128)}, u32[]{:S(2)}) %copy-start.3) | copy-done | bytes 88
  3.5 0.0 copy-start.4
  3.5 0.7 %copy-done.4 = s32[16]{0:T(128)S(1)} copy-done((s32[16]{0:T(128)S(1)}, s32[16]{0:T(128)}, u32[]{:S(2)}) %copy-start.4) | copy-done | bytes 88
  4.1 30.5 %contrastive.1 = (f32[16,1024]{1,0:T(8,128)S(1)}, f32[16,1024]{1,0:T(8,128)S(1)}, f32[1,128]{1,0:T(1,128)S(1)}) custom-call(bf16[16,1024]{1,0:T(8,128)(2,1)S(1)} %copy-done, bf16[16,1024]{1,0:T(8,128)(2,1)S(1)} %copy-done.1, s32[16]{0:T(128)S(1)} %copy-done.2, s32[16]{0:T(128)S(1)} %copy-done.3, s32[16]{0:T(128)S(1)} %copy-done.4), custom_call_target="tpu_custom_call" | custom-call | tf_op jit(solution)/shard_map/contrastive/pallas_call | solution.py:420
  34.6 0.5 %slice_bitcast_fusion = f32[16]{0:T(128)} fusion(f32[1,128]{1,0:T(1,128)S(1)} %get-tuple-element.8), kind=kLoop, calls=%fused_computation | loop fusion | bytes 128 | tf_op jit(solution)/shard_map/squeeze | solution.py:448
  35.1 0.6 %copy.10 = f32[16,1024]{1,0:T(8,128)} copy(f32[16,1024]{1,0:T(8,128)S(1)} %get-tuple-element.12) | data formatting | bytes 131072
  35.7 0.6 %copy.11 = f32[16,1024]{1,0:T(8,128)} copy(f32[16,1024]{1,0:T(8,128)S(1)} %get-tuple-element.13) | data formatting | bytes 131072
Async XLA Ops:
  0.6 0.8 %copy-start = (bf16[16,1024]{1,0:T(8,128)(2,1)S(1)}, bf16[16,1024]{1,0:T(8,128)(2,1)}, u32[]{:S(2)}) copy-start(bf16[16,1024]{1,0:T(8,128)(2,1)} %q_ref.1) | copy-start | bytes 98308
  1.4 0.8 %copy-start.1 = (bf16[16,1024]{1,0:T(8,128)(2,1)S(1)}, bf16[16,1024]{1,0:T(8,128)(2,1)}, u32[]{:S(2)}) copy-start(bf16[16,1024]{1,0:T(8,128)(2,1)} %p_ref.1) | copy-start | bytes 98308
  2.1 0.7 %copy-start.2 = (s32[16]{0:T(128)S(1)}, s32[16]{0:T(128)}, u32[]{:S(2)}) copy-start(s32[16]{0:T(128)} %pos_ref.1) | copy-start | bytes 196
  2.8 0.7 %copy-start.3 = (s32[16]{0:T(128)S(1)}, s32[16]{0:T(128)}, u32[]{:S(2)}) copy-start(s32[16]{0:T(128)} %qd_ref.1) | copy-start | bytes 196
  3.5 0.7 %copy-start.4 = (s32[16]{0:T(128)S(1)}, s32[16]{0:T(128)}, u32[]{:S(2)}) copy-start(s32[16]{0:T(128)} %pd_ref.1) | copy-start | bytes 196

commit v2 on v1

--- a/solution.py
+++ b/solution.py
@@ -164,18 +164,15 @@
     per_device,
     q_ref,
     p_ref,
-    pos_ref,
-    qd_ref,
-    pd_ref,
+    label_out,
     qg_ref,
     pg_ref,
     loss_ref,
+    scores_ref,
     rows,
-    label_out,
     labels,
     lse_out,
     lses,
-    load_sem,
     row_send,
     row_recv,
     label_send,
@@ -199,6 +196,7 @@
     sibling = (blk + 1 - 2 * core, inner)
     x_peer = (blk, inner + 1 - 2 * x)
     y_peer = ((1 - y) * 2 + core, inner)
+    diagonal_peer = (y_peer[0], x_peer[1])
 
     def block_of(device):
         return device[0] * inner_count + device[1]
@@ -212,13 +210,6 @@
     def half(block, k):
         start = pl.multiple_of(block * span + k * per_device, per_device)
         return rows.at[pl.ds(start, per_device)]
-
-    loads = [
-        pltpu.make_async_copy(q_ref, half(me, 0), load_sem.at[0]),
-        pltpu.make_async_copy(p_ref, half(me, 1), load_sem.at[1]),
-    ]
-    for copy in loads:
-        copy.start()
 
     barrier = pltpu.get_barrier_semaphore()
 
@@ -234,26 +225,9 @@
 
     lax.fori_loop(1, device_count, greet, 0)
 
-    lane = lax.broadcasted_iota(jnp.int32, (1, LANES), 1)
-    own_place = lax.div(lane, span) == lax.rem(me, per_lanes)
-    lane_here = lax.rem(lane, span)
-    code_row = jnp.zeros((1, LANES), jnp.int32)
-    dup_row = jnp.zeros((1, LANES), jnp.int32)
-    for k in range(per_device):
-        code_row = jnp.where(lane_here == k, pos_ref[k], code_row)
-        dup_row = jnp.where(lane_here == k, qd_ref[k], dup_row)
-        dup_row = jnp.where(lane_here == per_device + k, pd_ref[k], dup_row)
-    passage_lane = lane_here >= per_device
-    code_row = jnp.where(
-        passage_lane, me * per_device + lane_here - per_device + total_queries, code_row
-    )
-    label_out[0:1, :] = jnp.where(own_place, code_row, 0)
-    label_out[1:2, :] = jnp.where(own_place, dup_row, 0)
-
+    half(me, 0)[...] = q_ref[...]
+    half(me, 1)[...] = p_ref[...]
     pl.semaphore_wait(barrier, device_count - 1)
-    for copy in loads:
-        copy.wait()
-
     sent = []
 
     def send(ref, device, recv):
@@ -275,16 +249,21 @@
         send(whole(block), x_peer, row_recv.at[block, 0])
         send(whole(block), y_peer, row_recv.at[block, 0])
 
+    def send_diagonal(block):
+        send(whole(block), diagonal_peer, row_recv.at[block, 0])
+
     def to_sibling(block):
         send(whole(block), sibling, row_recv.at[block, 0])
 
-    spread(me)
+    for peer in (x_peer, y_peer):
+        send(whole(me), peer, row_recv.at[me, 0])
     for d in range(1, lines):
         send(whole(me), at_line((blk, inner), swapped(z, d)), row_recv.at[me, 0])
-    to_sibling(me)
-
-    own_labels = pltpu.make_async_copy(label_out, labels.at[me], label_recv)
-    own_labels.start()
+    send(whole(me), diagonal_peer, row_recv.at[me, 0])
+    send(whole(me), sibling, row_recv.at[me, 0])
+
+    own_label_copy = pltpu.make_async_copy(label_out, labels.at[me], label_recv)
+    own_label_copy.start()
 
     def send_small(out, into, send_sem, recv_sem):
         def step(d, carry):
@@ -303,27 +282,30 @@
 
     send_small(label_out, labels, label_send, label_recv)
 
-    for step in range(lines + 2):
-        if 1 <= step < lines:
-            block = block_of(at_line((blk, inner), swapped(z, step)))
-            arrived(whole(block), row_recv.at[block, 0])
-            spread(block)
-            to_sibling(block)
-        if 1 <= step <= lines:
-            there = swapped(z, step - 1)
-            block = block_of(at_line(x_peer, there))
-            arrived(whole(block), row_recv.at[block, 0])
-            send(half(block, 0), y_peer, row_recv.at[block, 0])
-            to_sibling(block)
-            block = block_of(at_line(y_peer, there))
-            arrived(whole(block), row_recv.at[block, 0])
-            send(half(block, 1), x_peer, row_recv.at[block, 1])
-            to_sibling(block)
-        if step >= 2:
-            block = block_of(at_line((y_peer[0], x_peer[1]), swapped(z, step - 2)))
+
+    forwarded = (1,)
+    events = [("line", 1), ("x", 0), ("y", 0)]
+    events += [("line", d) for d in range(2, lines)] + [("diagonal", 0)]
+    for d in range(1, lines):
+        events += [("x", d), ("y", d)] + ([("diagonal", d - 1)] if d > 1 else [])
+    events += [("diagonal", lines - 1)]
+    for kind, d in events:
+        peer = {"line": (blk, inner), "x": x_peer, "y": y_peer, "diagonal": diagonal_peer}[kind]
+        block = block_of(at_line(peer, swapped(z, d)))
+        if kind == "diagonal" and d in forwarded:
             arrived(half(block, 0), row_recv.at[block, 0])
             arrived(half(block, 1), row_recv.at[block, 1])
-            to_sibling(block)
+        else:
+            arrived(whole(block), row_recv.at[block, 0])
+        if kind == "line":
+            spread(block)
+            if d not in forwarded:
+                send_diagonal(block)
+        if kind == "x" and d in forwarded:
+            send(half(block, 0), y_peer, row_recv.at[block, 0])
+        if kind == "y" and d in forwarded:
+            send(half(block, 1), x_peer, row_recv.at[block, 1])
+        to_sibling(block)
 
     arrived(labels, label_recv)
     codes = [
@@ -347,16 +329,21 @@
     paired = code_col == partner_lanes
     allowed = (code_col != code_lanes) & ((dup_col != dup_lanes) | paired)
 
-    for z_there in range(lines):
-        for y_there in range(blk_count // 2):
-            for x_there in range(2):
-                block = block_of(((2 * y_there + 1 - core), z_there * 2 + x_there))
+    own = whole(me)[...]
+    chunk = inner_count * span
+    for part in (blk, sibling[0], y_peer[0], blk_count - 1 - blk):
+        if part is not blk and part is not y_peer[0]:
+            for there in range(inner_count):
+                block = part * inner_count + there
                 arrived(whole(block), row_recv.at[block, 0])
-
-    own = whole(me)[...]
-    scores = SCALE * lax.dot_general(
-        own, rows[...], (((1,), (1,)), ((), ())), preferred_element_type=jnp.float32
-    )
+        start = pl.multiple_of(part * chunk, chunk)
+        scores_ref[:, pl.ds(start, chunk)] = lax.dot_general(
+            own,
+            rows[pl.ds(start, chunk), :],
+            (((1,), (1,)), ((), ())),
+            preferred_element_type=jnp.float32,
+        )
+    scores = SCALE * scores_ref[...]
     masked = jnp.where(allowed, scores, NEGATIVE)
     top = jnp.max(masked, axis=1, keepdims=True)
     total = jnp.sum(jnp.where(allowed, jnp.exp(masked - top), 0.0), axis=1, keepdims=True)
@@ -409,14 +396,25 @@
     arrived(lses.at[pl.ds(0, device_count - 1)], lse_send)
 
 
+def label_tile(me, positive, query_dups, passage_dups, total_queries):
+    per_device = positive.shape[0]
+    span = 2 * per_device
+    passages = me * per_device + jnp.arange(per_device, dtype=jnp.int32) + total_queries
+    both = jnp.stack(
+        [jnp.concatenate([positive, passages]), jnp.concatenate([query_dups, passage_dups])]
+    )
+    place = jnp.arange(LANES, dtype=jnp.int32) // span == me % (LANES // span)
+    return jnp.where(place[None, :], jnp.tile(both, (1, LANES // span)), 0)
+
+
 def fused_body(blk_count, inner_count, queries, passages, positive, query_dups, passage_dups):
     per_device, width = queries.shape
     device_count = blk_count * inner_count
     span = 2 * per_device
-    sends = (inner_count // 2) * 9 + 8
+    sends = (inner_count // 2) * 10
     vmem = pl.BlockSpec(memory_space=pltpu.VMEM)
-    smem = pl.BlockSpec(memory_space=pltpu.SMEM)
-    hbm = pl.BlockSpec(memory_space=pl.ANY)
+    me = lax.axis_index("blk") * inner_count + lax.axis_index("inner")
+    labels = label_tile(me, positive, query_dups, passage_dups, device_count * per_device)
     query_grad, passage_grad, losses = pl.pallas_call(
         functools.partial(fused_kernel, blk_count, inner_count, per_device),
         out_shape=(
@@ -424,15 +422,14 @@
             jax.ShapeDtypeStruct((per_device, width), jnp.float32),
             jax.ShapeDtypeStruct((1, LANES), jnp.float32),
         ),
-        in_specs=[hbm, hbm, smem, smem, smem],
+        in_specs=[vmem] * 3,
         out_specs=[vmem, vmem, vmem],
         scratch_shapes=[
+            pltpu.VMEM((span, device_count * span), jnp.float32),
             pltpu.VMEM((device_count * span, width), jnp.bfloat16),
-            pltpu.VMEM((2, LANES), jnp.int32),
             pltpu.VMEM((device_count, 2, LANES), jnp.int32),
             pltpu.VMEM((1, LANES), jnp.float32),
             pltpu.VMEM((device_count, 1, LANES), jnp.float32),
-            pltpu.SemaphoreType.DMA((2,)),
             pltpu.SemaphoreType.DMA((sends,)),
             pltpu.SemaphoreType.DMA((device_count, 2)),
             pltpu.SemaphoreType.DMA,
@@ -444,7 +441,7 @@
             collective_id=0, has_side_effects=True, vmem_limit_bytes=32 * 1024 * 1024
         ),
         name="contrastive",
-    )(queries, passages, positive, query_dups, passage_dups)
+    )(queries, passages, labels)
     return query_grad, passage_grad, losses[0, :per_device]
 
 

time: 36.7 us -> 32.7 us (0.89)
  Pallas kernels: 30.5 us -> 28.4 us
  local copies, waits for them, and re-layouts: 5.24 us -> 3.27 us
    pallas_call x1, Pallas kernels: 30.5 us -> 28.4 us  [fused_body(): pl.pallas_call(functools.partial(fused_kernel, blk_count, inner_count, pe...]
    unnamed x12, local copies, waits for them, and re-layouts: 4.73 us -> 2.67 us
where the time goes in v2:
time: 32.7 us; the launch traced here: 32.5 us
  Pallas kernels  28.4 us (87%)
  local copies, waits for them, and re-layouts  3.27 us (10%)
  between operations  0.71 us (2%)
    pallas_call x1, Pallas kernels, fused_body(): pl.pallas_call(functools.partial(fused_kernel, blk_count, inner_count, pe...  28.4 us
    unnamed x12, local copies, waits for them, and re-layouts  2.67 us

profile of v2, /device:TPU:0, one launch (start us, length us, event | category | flops | bytes accessed | tf_op | source)
XLA Modules:
  0.0 32.5 jit_solution(6085907405456745603)
XLA Ops:
  0.6 0.0 copy-start
  0.7 0.0 copy-start.2
  0.7 0.0 copy-start.3
  0.7 0.0 copy-start.4
  0.7 0.6 %copy-done.2 = s32[16]{0:T(128)S(1)} copy-done((s32[16]{0:T(128)S(1)}, s32[16]{0:T(128)}, u32[]{:S(2)}) %copy-start.2) | copy-done | bytes 88
  1.3 0.0 copy-done.3
  1.3 0.0 copy-done.4
  1.4 0.1 add_bitcast_fusion
  1.5 0.1 tile.10
  1.5 0.0 copy-done
  1.5 0.0 copy-start.1
  1.6 0.8 %copy-done.1 = bf16[16,1024]{1,0:T(8,128)(2,1)S(1)} copy-done((bf16[16,1024]{1,0:T(8,128)(2,1)S(1)}, bf16[16,1024]{1,0:T(8,128)(2,1)}, u32[]{:S(2)}) %copy-start.1) | copy-done | bytes 32792
  2.3 28.4 %contrastive.1 = (f32[16,1024]{1,0:T(8,128)S(1)}, f32[16,1024]{1,0:T(8,128)S(1)}, f32[1,128]{1,0:T(1,128)S(1)}) custom-call(bf16[16,1024]{1,0:T(8,128)(2,1)S(1)} %copy-done, bf16[16,1024]{1,0:T(8,128)(2,1)S(1)} %copy-done.1, s32[2,128]{1,0:T(2,128)S(1)} %broadcast_select_fusion.label_out), custom_call_target="tpu_custom_call" | custom-call | tf_op jit(solution)/shard_map/contrastive/pallas_call | solution.py:418
  30.7 0.5 %slice_bitcast_fusion = f32[16]{0:T(128)} fusion(f32[1,128]{1,0:T(1,128)S(1)} %get-tuple-element.8), kind=kLoop, calls=%fused_computation.9 | loop fusion | bytes 128 | tf_op jit(solution)/shard_map/squeeze | solution.py:445
  31.2 0.6 %copy.10 = f32[16,1024]{1,0:T(8,128)} copy(f32[16,1024]{1,0:T(8,128)S(1)} %get-tuple-element.14) | data formatting | bytes 131072
  31.9 0.6 %copy.11 = f32[16,1024]{1,0:T(8,128)} copy(f32[16,1024]{1,0:T(8,128)S(1)} %get-tuple-element.15) | data formatting | bytes 131072
  (5 shorter events, 0.0 us)
Async XLA Ops:
  0.6 0.9 %copy-start = (bf16[16,1024]{1,0:T(8,128)(2,1)S(1)}, bf16[16,1024]{1,0:T(8,128)(2,1)}, u32[]{:S(2)}) copy-start(bf16[16,1024]{1,0:T(8,128)(2,1)} %q_ref.1) | copy-start | bytes 98308
  0.7 0.7 %copy-start.2 = (s32[16]{0:T(128)S(1)}, s32[16]{0:T(128)}, u32[]{:S(2)}) copy-start(s32[16]{0:T(128)} %param.7) | copy-start | bytes 196
  0.7 0.7 %copy-start.3 = (s32[16]{0:T(128)S(1)}, s32[16]{0:T(128)}, u32[]{:S(2)}) copy-start(s32[16]{0:T(128)} %param.9) | copy-start | bytes 196
  0.7 0.7 %copy-start.4 = (s32[16]{0:T(128)S(1)}, s32[16]{0:T(128)}, u32[]{:S(2)}) copy-start(s32[16]{0:T(128)} %param.8) | copy-start | bytes 196
  1.5 0.8 %copy-start.1 = (bf16[16,1024]{1,0:T(8,128)(2,1)S(1)}, bf16[16,1024]{1,0:T(8,128)(2,1)}, u32[]{:S(2)}) copy-start(bf16[16,1024]{1,0:T(8,128)(2,1)} %p_ref.1) | copy-start | bytes 98308

commit v3 on v2

--- a/solution.py
+++ b/solution.py
@@ -165,8 +165,7 @@
     q_ref,
     p_ref,
     label_out,
-    qg_ref,
-    pg_ref,
+    grad_ref,
     loss_ref,
     scores_ref,
     rows,
@@ -283,28 +282,23 @@
     send_small(label_out, labels, label_send, label_recv)
 
 
-    forwarded = (1,)
-    events = [("line", 1), ("x", 0), ("y", 0)]
-    events += [("line", d) for d in range(2, lines)] + [("diagonal", 0)]
+    along_z = [d for d in range(1, lines) if d in (1,3)]
+    events = [("line", 1), ("x", 0), ("y", 0), ("diagonal", 0)]
+    events += [("line", d) for d in range(2, lines)]
     for d in range(1, lines):
-        events += [("x", d), ("y", d)] + ([("diagonal", d - 1)] if d > 1 else [])
-    events += [("diagonal", lines - 1)]
+        events += [("x", d), ("y", d), ("diagonal", d)]
     for kind, d in events:
         peer = {"line": (blk, inner), "x": x_peer, "y": y_peer, "diagonal": diagonal_peer}[kind]
         block = block_of(at_line(peer, swapped(z, d)))
-        if kind == "diagonal" and d in forwarded:
-            arrived(half(block, 0), row_recv.at[block, 0])
-            arrived(half(block, 1), row_recv.at[block, 1])
-        else:
-            arrived(whole(block), row_recv.at[block, 0])
+        arrived(whole(block), row_recv.at[block, 0])
         if kind == "line":
             spread(block)
-            if d not in forwarded:
+            if d not in along_z:
                 send_diagonal(block)
-        if kind == "x" and d in forwarded:
-            send(half(block, 0), y_peer, row_recv.at[block, 0])
-        if kind == "y" and d in forwarded:
-            send(half(block, 1), x_peer, row_recv.at[block, 1])
+        if kind == "diagonal" and d == 0:
+            for far in along_z:
+                there = at_line((blk, inner), swapped(z, far))
+                send(whole(block), there, row_recv.at[block, 0])
         to_sibling(block)
 
     arrived(labels, label_recv)
@@ -381,14 +375,13 @@
     loss_ref[...] = jnp.sum(jnp.where(place, losses, 0.0), axis=0, keepdims=True)
     mixed = jnp.exp(masked - pair_col) + jnp.exp(masked - pair_lanes)
     weights = jnp.where(allowed, mixed, 0.0) - paired.astype(jnp.float32)
-    gradient = SCALE * lax.dot_general(
+    gradient = lax.dot_general(
         weights.astype(jnp.bfloat16),
         rows[...],
         (((1,), (0,)), ((), ())),
         preferred_element_type=jnp.float32,
     )
-    qg_ref[...] = gradient[:per_device]
-    pg_ref[...] = gradient[per_device:]
+    grad_ref[...] = gradient
 
     for copy in sent:
         copy.wait_send()
@@ -415,15 +408,14 @@
     vmem = pl.BlockSpec(memory_space=pltpu.VMEM)
     me = lax.axis_index("blk") * inner_count + lax.axis_index("inner")
     labels = label_tile(me, positive, query_dups, passage_dups, device_count * per_device)
-    query_grad, passage_grad, losses = pl.pallas_call(
+    gradient, losses = pl.pallas_call(
         functools.partial(fused_kernel, blk_count, inner_count, per_device),
         out_shape=(
-            jax.ShapeDtypeStruct((per_device, width), jnp.float32),
-            jax.ShapeDtypeStruct((per_device, width), jnp.float32),
+            jax.ShapeDtypeStruct((span, width), jnp.float32),
             jax.ShapeDtypeStruct((1, LANES), jnp.float32),
         ),
         in_specs=[vmem] * 3,
-        out_specs=[vmem, vmem, vmem],
+        out_specs=[vmem, vmem],
         scratch_shapes=[
             pltpu.VMEM((span, device_count * span), jnp.float32),
             pltpu.VMEM((device_count * span, width), jnp.bfloat16),
@@ -442,7 +434,7 @@
         ),
         name="contrastive",
     )(queries, passages, labels)
-    return query_grad, passage_grad, losses[0, :per_device]
+    return SCALE * gradient[:per_device], SCALE * gradient[per_device:], losses[0, :per_device]
 
 
 def solution(mesh):

time: 32.7 us -> 30.1 us (0.920)
  Pallas kernels: 28.4 us -> 26.4 us
  local copies, waits for them, and re-layouts: 3.27 us -> 2.01 us
  other arithmetic: 0.11 us -> 0.77 us
    pallas_call x1, Pallas kernels: 28.4 us -> 26.4 us  [fused_body(): pl.pallas_call(functools.partial(fused_kernel, blk_count, inner_count, pe...]
    unnamed x12 -> x10, local copies, waits for them, and re-layouts: 2.67 us -> 1.41 us
    mul x0 -> x1, other arithmetic: none -> 0.66 us  [fused_body(): SCALE * gradient[per_device:]]
where the time goes in v3:
time: 30.1 us; the launch traced here: 29.9 us
  Pallas kernels  26.4 us (88%)
  local copies, waits for them, and re-layouts  2.01 us (7%)
  other arithmetic  0.77 us (3%)
  between operations  0.71 us (2%)
    pallas_call x1, Pallas kernels, fused_body(): pl.pallas_call(functools.partial(fused_kernel, blk_count, inner_count, pe...  26.4 us
    unnamed x10, local copies, waits for them, and re-layouts  1.41 us
    mul x1, other arithmetic, fused_body(): SCALE * gradient[per_device:]  0.66 us

profile of v3, /device:TPU:0, one launch (start us, length us, event | category | flops | bytes accessed | tf_op | source)
XLA Modules:
  0.0 29.9 jit_solution(5489718620137202707)
XLA Ops:
  0.6 0.0 copy-start
  0.7 0.0 copy-start.2
  0.7 0.0 copy-start.3
  0.7 0.0 copy-start.4
  0.7 0.6 %copy-done.2 = s32[16]{0:T(128)S(1)} copy-done((s32[16]{0:T(128)S(1)}, s32[16]{0:T(128)}, u32[]{:S(2)}) %copy-start.2) | copy-done | bytes 88
  1.3 0.0 copy-done.3
  1.3 0.0 copy-done.4
  1.4 0.1 add_bitcast_fusion
  1.5 0.1 tile.10
  1.5 0.0 copy-done
  1.5 0.0 copy-start.1
  1.6 0.8 %copy-done.1 = bf16[16,1024]{1,0:T(8,128)(2,1)S(1)} copy-done((bf16[16,1024]{1,0:T(8,128)(2,1)S(1)}, bf16[16,1024]{1,0:T(8,128)(2,1)}, u32[]{:S(2)}) %copy-start.1) | copy-done | bytes 32792
  2.3 26.4 %contrastive.1 = (f32[32,1024]{1,0:T(8,128)S(1)}, f32[1,128]{1,0:T(1,128)S(1)}) custom-call(bf16[16,1024]{1,0:T(8,128)(2,1)S(1)} %copy-done, bf16[16,1024]{1,0:T(8,128)(2,1)S(1)} %copy-done.1, s32[2,128]{1,0:T(2,128)S(1)} %broadcast_select_fusion.label_out), custom_call_target="tpu_custom_call" | custom-call | tf_op jit(solution)/shard_map/contrastive/pallas_call | solution.py:411
  28.7 0.7 %slice_multiply_fusion = (f32[16,1024]{1,0:T(8,128)}, f32[16,1024]{1,0:T(8,128)}) fusion(f32[32,1024]{1,0:T(8,128)S(1)} %get-tuple-element.5), kind=kLoop, calls=%fused_computation | loop fusion | flops 32768 | bytes 262144 | tf_op jit(solution)/shard_map/mul | solution.py:437
  29.4 0.5 %slice_bitcast_fusion = f32[16]{0:T(128)} fusion(f32[1,128]{1,0:T(1,128)S(1)} %get-tuple-element.6), kind=kLoop, calls=%fused_computation.11 | loop fusion | bytes 128 | tf_op jit(solution)/shard_map/squeeze | solution.py:437
  (5 shorter events, 0.0 us)
Async XLA Ops:
  0.6 0.9 %copy-start = (bf16[16,1024]{1,0:T(8,128)(2,1)S(1)}, bf16[16,1024]{1,0:T(8,128)(2,1)}, u32[]{:S(2)}) copy-start(bf16[16,1024]{1,0:T(8,128)(2,1)} %q_ref.1) | copy-start | bytes 98308
  0.7 0.7 %copy-start.2 = (s32[16]{0:T(128)S(1)}, s32[16]{0:T(128)}, u32[]{:S(2)}) copy-start(s32[16]{0:T(128)} %param.7) | copy-start | bytes 196
  0.7 0.7 %copy-start.3 = (s32[16]{0:T(128)S(1)}, s32[16]{0:T(128)}, u32[]{:S(2)}) copy-start(s32[16]{0:T(128)} %param.9) | copy-start | bytes 196
  0.7 0.7 %copy-start.4 = (s32[16]{0:T(128)S(1)}, s32[16]{0:T(128)}, u32[]{:S(2)}) copy-start(s32[16]{0:T(128)} %param.8) | copy-start | bytes 196
  1.5 0.8 %copy-start.1 = (bf16[16,1024]{1,0:T(8,128)(2,1)S(1)}, bf16[16,1024]{1,0:T(8,128)(2,1)}, u32[]{:S(2)}) copy-start(bf16[16,1024]{1,0:T(8,128)(2,1)} %p_ref.1) | copy-start | bytes 98308

commit v4 on v3

--- a/solution.py
+++ b/solution.py
@@ -174,8 +174,6 @@
     lses,
     row_send,
     row_recv,
-    label_send,
-    label_recv,
     lse_send,
     lse_recv,
 ):
@@ -212,57 +210,53 @@
 
     barrier = pltpu.get_barrier_semaphore()
 
-    def greet(d, carry):
-        target = lax.rem(me + d, device_count)
+    peers = [x_peer, y_peer, diagonal_peer, sibling]
+    peers += [at_line((blk, inner), swapped(z, d)) for d in range(1, lines)]
+    for peer in peers:
         pl.semaphore_signal(
-            barrier,
-            inc=1,
-            device_id=(lax.div(target, inner_count), lax.rem(target, inner_count)),
-            device_id_type=pl.DeviceIdType.MESH,
+            barrier, inc=1, device_id=peer, device_id_type=pl.DeviceIdType.MESH
         )
-        return carry
-
-    lax.fori_loop(1, device_count, greet, 0)
-
+    labels[me] = label_out[...]
     half(me, 0)[...] = q_ref[...]
     half(me, 1)[...] = p_ref[...]
-    pl.semaphore_wait(barrier, device_count - 1)
+    pl.semaphore_wait(barrier, len(peers))
     sent = []
 
-    def send(ref, device, recv):
-        copy = pltpu.make_async_remote_copy(
-            src_ref=ref,
-            dst_ref=ref,
-            send_sem=row_send.at[len(sent)],
-            recv_sem=recv,
-            device_id=device,
-            device_id_type=pl.DeviceIdType.MESH,
-        )
-        copy.start()
-        sent.append(copy)
+    def send(block, device):
+        for ref, recv in (
+            (labels.at[block], row_recv.at[block, 1]),
+            (whole(block), row_recv.at[block, 0]),
+        ):
+            copy = pltpu.make_async_remote_copy(
+                src_ref=ref,
+                dst_ref=ref,
+                send_sem=row_send.at[len(sent)],
+                recv_sem=recv,
+                device_id=device,
+                device_id_type=pl.DeviceIdType.MESH,
+            )
+            copy.start()
+            sent.append(copy)
 
     def arrived(ref, sem):
         pltpu.make_async_copy(ref, ref, sem).wait()
 
     def spread(block):
-        send(whole(block), x_peer, row_recv.at[block, 0])
-        send(whole(block), y_peer, row_recv.at[block, 0])
+        send(block, x_peer)
+        send(block, y_peer)
 
     def send_diagonal(block):
-        send(whole(block), diagonal_peer, row_recv.at[block, 0])
+        send(block, diagonal_peer)
 
     def to_sibling(block):
-        send(whole(block), sibling, row_recv.at[block, 0])
+        send(block, sibling)
 
     for peer in (x_peer, y_peer):
-        send(whole(me), peer, row_recv.at[me, 0])
+        send(me, peer)
     for d in range(1, lines):
-        send(whole(me), at_line((blk, inner), swapped(z, d)), row_recv.at[me, 0])
-    send(whole(me), diagonal_peer, row_recv.at[me, 0])
-    send(whole(me), sibling, row_recv.at[me, 0])
-
-    own_label_copy = pltpu.make_async_copy(label_out, labels.at[me], label_recv)
-    own_label_copy.start()
+        send(me, at_line((blk, inner), swapped(z, d)))
+    send(me, diagonal_peer)
+    send(me, sibling)
 
     def send_small(out, into, send_sem, recv_sem):
         def step(d, carry):
@@ -279,8 +273,6 @@
 
         lax.fori_loop(1, device_count, step, 0)
 
-    send_small(label_out, labels, label_send, label_recv)
-
 
     along_z = [d for d in range(1, lines) if d in (1,3)]
     events = [("line", 1), ("x", 0), ("y", 0), ("diagonal", 0)]
@@ -290,6 +282,7 @@
     for kind, d in events:
         peer = {"line": (blk, inner), "x": x_peer, "y": y_peer, "diagonal": diagonal_peer}[kind]
         block = block_of(at_line(peer, swapped(z, d)))
+        arrived(labels.at[block], row_recv.at[block, 1])
         arrived(whole(block), row_recv.at[block, 0])
         if kind == "line":
             spread(block)
@@ -298,10 +291,24 @@
         if kind == "diagonal" and d == 0:
             for far in along_z:
                 there = at_line((blk, inner), swapped(z, far))
-                send(whole(block), there, row_recv.at[block, 0])
+                send(block, there)
         to_sibling(block)
 
-    arrived(labels, label_recv)
+    own = whole(me)[...]
+    chunk = inner_count * span
+    for part in (blk, sibling[0], y_peer[0], blk_count - 1 - blk):
+        if part is not blk and part is not y_peer[0]:
+            for there in range(inner_count):
+                block = part * inner_count + there
+                arrived(labels.at[block], row_recv.at[block, 1])
+                arrived(whole(block), row_recv.at[block, 0])
+        start = pl.multiple_of(part * chunk, chunk)
+        scores_ref[:, pl.ds(start, chunk)] = lax.dot_general(
+            own,
+            rows[pl.ds(start, chunk), :],
+            (((1,), (1,)), ((), ())),
+            preferred_element_type=jnp.float32,
+        )
     codes = [
         lane_sum([labels[g * per_lanes + k][0:1, :] for k in range(per_lanes)])
         for g in range(groups)
@@ -323,20 +330,6 @@
     paired = code_col == partner_lanes
     allowed = (code_col != code_lanes) & ((dup_col != dup_lanes) | paired)
 
-    own = whole(me)[...]
-    chunk = inner_count * span
-    for part in (blk, sibling[0], y_peer[0], blk_count - 1 - blk):
-        if part is not blk and part is not y_peer[0]:
-            for there in range(inner_count):
-                block = part * inner_count + there
-                arrived(whole(block), row_recv.at[block, 0])
-        start = pl.multiple_of(part * chunk, chunk)
-        scores_ref[:, pl.ds(start, chunk)] = lax.dot_general(
-            own,
-            rows[pl.ds(start, chunk), :],
-            (((1,), (1,)), ((), ())),
-            preferred_element_type=jnp.float32,
-        )
     scores = SCALE * scores_ref[...]
     masked = jnp.where(allowed, scores, NEGATIVE)
     top = jnp.max(masked, axis=1, keepdims=True)
@@ -385,7 +378,6 @@
 
     for copy in sent:
         copy.wait_send()
-    arrived(labels.at[pl.ds(0, device_count - 1)], label_send)
     arrived(lses.at[pl.ds(0, device_count - 1)], lse_send)
 
 
@@ -404,7 +396,7 @@
     per_device, width = queries.shape
     device_count = blk_count * inner_count
     span = 2 * per_device
-    sends = (inner_count // 2) * 10
+    sends = (inner_count // 2) * 20
     vmem = pl.BlockSpec(memory_space=pltpu.VMEM)
     me = lax.axis_index("blk") * inner_count + lax.axis_index("inner")
     labels = label_tile(me, positive, query_dups, passage_dups, device_count * per_device)
@@ -426,8 +418,6 @@
             pltpu.SemaphoreType.DMA((device_count, 2)),
             pltpu.SemaphoreType.DMA,
             pltpu.SemaphoreType.DMA,
-            pltpu.SemaphoreType.DMA,
-            pltpu.SemaphoreType.DMA,
         ],
         compiler_params=pltpu.CompilerParams(
             collective_id=0, has_side_effects=True, vmem_limit_bytes=32 * 1024 * 1024

time: 30.1 us -> 28.9 us (0.960)
  Pallas kernels: 26.4 us -> 25.2 us
    pallas_call x1, Pallas kernels: 26.4 us -> 25.2 us  [fused_body(): pl.pallas_call(functools.partial(fused_kernel, blk_count, inner_count, pe...]
where the time goes in v4:
time: 28.9 us; the launch traced here: 28.7 us
  Pallas kernels  25.2 us (87%)
  local copies, waits for them, and re-layouts  2.01 us (7%)
  other arithmetic  0.77 us (3%)
  between operations  0.71 us (2%)
    pallas_call x1, Pallas kernels, fused_body(): pl.pallas_call(functools.partial(fused_kernel, blk_count, inner_count, pe...  25.2 us
    unnamed x10, local copies, waits for them, and re-layouts  1.41 us
    mul x1, other arithmetic, fused_body(): SCALE * gradient[per_device:]  0.66 us

profile of v4, /device:TPU:0, one launch (start us, length us, event | category | flops | bytes accessed | tf_op | source)
XLA Modules:
  0.0 28.7 jit_solution(9925907443930328219)
XLA Ops:
  0.6 0.0 copy-start
  0.7 0.0 copy-start.2
  0.7 0.0 copy-start.3
  0.7 0.0 copy-start.4
  0.7 0.6 %copy-done.2 = s32[16]{0:T(128)S(1)} copy-done((s32[16]{0:T(128)S(1)}, s32[16]{0:T(128)}, u32[]{:S(2)}) %copy-start.2) | copy-done | bytes 88
  1.3 0.0 copy-done.3
  1.3 0.0 copy-done.4
  1.4 0.1 add_bitcast_fusion
  1.5 0.1 tile.10
  1.5 0.0 copy-done
  1.5 0.0 copy-start.1
  1.6 0.8 %copy-done.1 = bf16[16,1024]{1,0:T(8,128)(2,1)S(1)} copy-done((bf16[16,1024]{1,0:T(8,128)(2,1)S(1)}, bf16[16,1024]{1,0:T(8,128)(2,1)}, u32[]{:S(2)}) %copy-start.1) | copy-done | bytes 32792
  2.3 25.2 %contrastive.1 = (f32[32,1024]{1,0:T(8,128)S(1)}, f32[1,128]{1,0:T(1,128)S(1)}) custom-call(bf16[16,1024]{1,0:T(8,128)(2,1)S(1)} %copy-done, bf16[16,1024]{1,0:T(8,128)(2,1)S(1)} %copy-done.1, s32[2,128]{1,0:T(2,128)S(1)} %broadcast_select_fusion.label_out), custom_call_target="tpu_custom_call" | custom-call | tf_op jit(solution)/shard_map/contrastive/pallas_call | solution.py:403
  27.5 0.7 %slice_multiply_fusion = (f32[16,1024]{1,0:T(8,128)}, f32[16,1024]{1,0:T(8,128)}) fusion(f32[32,1024]{1,0:T(8,128)S(1)} %get-tuple-element.5), kind=kLoop, calls=%fused_computation | loop fusion | flops 32768 | bytes 262144 | tf_op jit(solution)/shard_map/mul | solution.py:427
  28.2 0.5 %slice_bitcast_fusion = f32[16]{0:T(128)} fusion(f32[1,128]{1,0:T(1,128)S(1)} %get-tuple-element.6), kind=kLoop, calls=%fused_computation.11 | loop fusion | bytes 128 | tf_op jit(solution)/shard_map/squeeze | solution.py:427
  (5 shorter events, 0.0 us)
Async XLA Ops:
  0.6 0.9 %copy-start = (bf16[16,1024]{1,0:T(8,128)(2,1)S(1)}, bf16[16,1024]{1,0:T(8,128)(2,1)}, u32[]{:S(2)}) copy-start(bf16[16,1024]{1,0:T(8,128)(2,1)} %q_ref.1) | copy-start | bytes 98308
  0.7 0.7 %copy-start.2 = (s32[16]{0:T(128)S(1)}, s32[16]{0:T(128)}, u32[]{:S(2)}) copy-start(s32[16]{0:T(128)} %param.7) | copy-start | bytes 196
  0.7 0.7 %copy-start.3 = (s32[16]{0:T(128)S(1)}, s32[16]{0:T(128)}, u32[]{:S(2)}) copy-start(s32[16]{0:T(128)} %param.9) | copy-start | bytes 196
  0.7 0.7 %copy-start.4 = (s32[16]{0:T(128)S(1)}, s32[16]{0:T(128)}, u32[]{:S(2)}) copy-start(s32[16]{0:T(128)} %param.8) | copy-start | bytes 196
  1.5 0.8 %copy-start.1 = (bf16[16,1024]{1,0:T(8,128)(2,1)S(1)}, bf16[16,1024]{1,0:T(8,128)(2,1)}, u32[]{:S(2)}) copy-start(bf16[16,1024]{1,0:T(8,128)(2,1)} %p_ref.1) | copy-start | bytes 98308

commit v5 on v4

--- a/solution.py
+++ b/solution.py
@@ -296,12 +296,8 @@
 
     own = whole(me)[...]
     chunk = inner_count * span
-    for part in (blk, sibling[0], y_peer[0], blk_count - 1 - blk):
-        if part is not blk and part is not y_peer[0]:
-            for there in range(inner_count):
-                block = part * inner_count + there
-                arrived(labels.at[block], row_recv.at[block, 1])
-                arrived(whole(block), row_recv.at[block, 0])
+
+    def score_part(part):
         start = pl.multiple_of(part * chunk, chunk)
         scores_ref[:, pl.ds(start, chunk)] = lax.dot_general(
             own,
@@ -309,6 +305,14 @@
             (((1,), (1,)), ((), ())),
             preferred_element_type=jnp.float32,
         )
+
+    score_part(blk)
+    score_part(y_peer[0])
+    sibling_parts = (sibling[0], blk_count - 1 - blk)
+    for part in sibling_parts:
+        for there in range(inner_count):
+            block = part * inner_count + there
+            arrived(labels.at[block], row_recv.at[block, 1])
     codes = [
         lane_sum([labels[g * per_lanes + k][0:1, :] for k in range(per_lanes)])
         for g in range(groups)
@@ -330,6 +334,11 @@
     paired = code_col == partner_lanes
     allowed = (code_col != code_lanes) & ((dup_col != dup_lanes) | paired)
 
+    for part in sibling_parts:
+        for there in range(inner_count):
+            block = part * inner_count + there
+            arrived(whole(block), row_recv.at[block, 0])
+        score_part(part)
     scores = SCALE * scores_ref[...]
     masked = jnp.where(allowed, scores, NEGATIVE)
     top = jnp.max(masked, axis=1, keepdims=True)

time: 28.9 us -> 29.1 us (level)
  no operation moved by 1% of the time
where the time goes in v5:
time: 29.1 us; the launch traced here: 28.8 us
  Pallas kernels  25.3 us (87%)
  local copies, waits for them, and re-layouts  2.01 us (7%)
  other arithmetic  0.77 us (3%)
  between operations  0.71 us (2%)
    pallas_call x1, Pallas kernels, fused_body(): pl.pallas_call(functools.partial(fused_kernel, blk_count, inner_count, pe...  25.3 us
    unnamed x10, local copies, waits for them, and re-layouts  1.41 us
    mul x1, other arithmetic, fused_body(): SCALE * gradient[per_device:]  0.66 us

profile of v5, /device:TPU:0, one launch (start us, length us, event | category | flops | bytes accessed | tf_op | source)
XLA Modules:
  0.0 28.8 jit_solution(11629645894535215223)
XLA Ops:
  0.6 0.0 copy-start
  0.7 0.0 copy-start.2
  0.7 0.0 copy-start.3
  0.7 0.0 copy-start.4
  0.7 0.6 %copy-done.2 = s32[16]{0:T(128)S(1)} copy-done((s32[16]{0:T(128)S(1)}, s32[16]{0:T(128)}, u32[]{:S(2)}) %copy-start.2) | copy-done | bytes 88
  1.3 0.0 copy-done.3
  1.3 0.0 copy-done.4
  1.4 0.1 add_bitcast_fusion
  1.5 0.1 tile.10
  1.5 0.0 copy-done
  1.5 0.0 copy-start.1
  1.6 0.8 %copy-done.1 = bf16[16,1024]{1,0:T(8,128)(2,1)S(1)} copy-done((bf16[16,1024]{1,0:T(8,128)(2,1)S(1)}, bf16[16,1024]{1,0:T(8,128)(2,1)}, u32[]{:S(2)}) %copy-start.1) | copy-done | bytes 32792
  2.3 25.3 %contrastive.1 = (f32[32,1024]{1,0:T(8,128)S(1)}, f32[1,128]{1,0:T(1,128)S(1)}) custom-call(bf16[16,1024]{1,0:T(8,128)(2,1)S(1)} %copy-done, bf16[16,1024]{1,0:T(8,128)(2,1)S(1)} %copy-done.1, s32[2,128]{1,0:T(2,128)S(1)} %broadcast_select_fusion.label_out), custom_call_target="tpu_custom_call" | custom-call | tf_op jit(solution)/shard_map/contrastive/pallas_call | solution.py:412
  27.7 0.7 %slice_multiply_fusion = (f32[16,1024]{1,0:T(8,128)}, f32[16,1024]{1,0:T(8,128)}) fusion(f32[32,1024]{1,0:T(8,128)S(1)} %get-tuple-element.5), kind=kLoop, calls=%fused_computation | loop fusion | flops 32768 | bytes 262144 | tf_op jit(solution)/shard_map/mul | solution.py:436
  28.3 0.5 %slice_bitcast_fusion = f32[16]{0:T(128)} fusion(f32[1,128]{1,0:T(1,128)S(1)} %get-tuple-element.6), kind=kLoop, calls=%fused_computation.11 | loop fusion | bytes 128 | tf_op jit(solution)/shard_map/squeeze | solution.py:436
  (5 shorter events, 0.0 us)
Async XLA Ops:
  0.6 0.9 %copy-start = (bf16[16,1024]{1,0:T(8,128)(2,1)S(1)}, bf16[16,1024]{1,0:T(8,128)(2,1)}, u32[]{:S(2)}) copy-start(bf16[16,1024]{1,0:T(8,128)(2,1)} %q_ref.1) | copy-start | bytes 98308
  0.7 0.7 %copy-start.2 = (s32[16]{0:T(128)S(1)}, s32[16]{0:T(128)}, u32[]{:S(2)}) copy-start(s32[16]{0:T(128)} %param.7) | copy-start | bytes 196
  0.7 0.7 %copy-start.3 = (s32[16]{0:T(128)S(1)}, s32[16]{0:T(128)}, u32[]{:S(2)}) copy-start(s32[16]{0:T(128)} %param.9) | copy-start | bytes 196
  0.7 0.7 %copy-start.4 = (s32[16]{0:T(128)S(1)}, s32[16]{0:T(128)}, u32[]{:S(2)}) copy-start(s32[16]{0:T(128)} %param.8) | copy-start | bytes 196
  1.5 0.8 %copy-start.1 = (bf16[16,1024]{1,0:T(8,128)(2,1)S(1)}, bf16[16,1024]{1,0:T(8,128)(2,1)}, u32[]{:S(2)}) copy-start(bf16[16,1024]{1,0:T(8,128)(2,1)} %p_ref.1) | copy-start | bytes 98308
